TPU v7x, 32 devices: a whole 2x2x4 slice. The times are simulated.
32 devices in a mesh: row: 16 (over z, y, core), col: 2 (over x).
Axes of the slice: x: 2, y: 2, z: 4, core: 2. Of those that a mesh axis runs over, the one named last changes fastest.
Arguments:
- inverse_tiles: bfloat16 [128, 256, 128, 256], P('col', None, 'row'), may hold values from -6 to 6
- factor_panels: bfloat16 [2, 128, 256, 256], P(None, 'row', 'col'), may hold values from -0.0390625 to 0.0390625
- ancestors: int32 [2, 96], replicated, may hold values from 0 to 127, as said below
- valid_flags: int32 [2, 96], replicated, may hold values from 0 to 1, as said below
- block_slot: int32 [128], replicated, may hold values from 0 to 127, each once
Outputs:
- new_panels: float32 [128, 256, 2, 256], P('col', 'row')
Inputs may be any that keep to these rules, and one draw needn't show every extreme that they name: `ancestors`: within one supernode's list all 96 entries name different blocks. `valid_flags`: each list's used entries come first; supernode 0's list is used in full, the others in 64 entries or more.
All inputs are finite; a program needn't handle non-finite values.
Results may differ from a plain program's by a relative error of at most 0.0003.
Values may be sent and summed in bfloat16 or wider, within the bound.
A program may use at most 256 MiB of HBM per device.

v0:
```python
import jax
import jax.numpy as jnp
from jax import lax
from jax.sharding import PartitionSpec as P


def membership(ancestors, valid_flags, block_slot):
    blocks = jnp.arange(block_slot.shape[0], dtype=jnp.int32)
    pick = (ancestors[:, :, None] == blocks[None, None, :]).astype(jnp.int32)
    slots = jnp.sum(pick * block_slot[None, None, :], axis=2)
    hits = (slots[:, :, None] == blocks[None, None, :]) & (valid_flags[:, :, None] == 1)
    return jnp.any(hits, axis=1)


def panel_product(left, right):
    return jnp.dot(left, right, preferred_element_type=jnp.float32)


def per_device(inverse_tiles, factor_panels, ancestors, valid_flags, block_slot):
    local_rows = inverse_tiles.shape[0]
    width = inverse_tiles.shape[1]
    local_cols = inverse_tiles.shape[2]
    panel_count = factor_panels.shape[0]
    member = membership(ancestors, valid_flags, block_slot)
    col_start = lax.axis_index("row") * local_cols
    row_start = lax.axis_index("col") * local_rows
    col_member = lax.dynamic_slice_in_dim(member, col_start, local_cols, 1)
    row_member = lax.dynamic_slice_in_dim(member, row_start, local_rows, 1)
    left = inverse_tiles.reshape(local_rows * width, local_cols * width)
    masked_local = jnp.where(
        col_member[:, :, None, None], factor_panels, jnp.zeros((), factor_panels.dtype)
    )
    results = []
    for which in range(panel_count):
        whole = lax.all_gather(masked_local[which], "col", axis=1, tiled=True)
        right = whole.reshape(local_cols * width, width)
        partial_value = panel_product(left, right)
        summed = lax.psum_scatter(
            partial_value.reshape(local_rows, width, width), "row", scatter_dimension=1, tiled=True
        )
        results.append(summed)
    stacked = jnp.stack(results, axis=2)
    rowmask = jnp.transpose(row_member)[:, None, :, None]
    return jnp.where(rowmask, -stacked, jnp.zeros((), jnp.float32))


def solution(mesh):
    return jax.shard_map(
        per_device,
        mesh=mesh,
        in_specs=(P("col", None, "row", None), P(None, "row", "col", None), P(), P(), P()),
        out_specs=P("col", "row", None, None),
        check_vma=False,
    )
```

profile of v0, /device:TPU:0, one launch (start us, length us, event | category | flops | bytes accessed | tf_op | source)
XLA Modules:
  0.0 480.9 jit_solution(909476461882325794)
XLA Ops:
  6.5 0.0 all-gather.5.cloned.1.call-start
  6.5 0.7 broadcast_compare_fusion
  7.2 0.9 select_reduce_fusion
  8.1 0.1 fusion.2
  8.2 0.1 constant_dynamic-slice_fusion
  8.3 1.4 broadcast_select_fusion
  9.7 1.1 fusion.3
  10.8 0.0 all-gather.5.cloned.1.call-update
  10.8 0.0 all-gather.7.cloned.1.call-start
  10.8 0.7 all-gather.7.cloned.1.call-update
  11.6 0.0 reduce-scatter.3.cloned.1.call-start
  11.6 44.9 %copy.17 = bf16[2048,8,8,256]{3,1,2,0:T(8,128)(2,1)} copy(bf16[2048,8,8,256]{3,2,1,0:T(8,128)(2,1)} %bitcast.10) | data formatting | bytes 134217728
  56.5 0.0 all-gather.5.cloned.1.call-done
  56.5 32.5 %convolution_bitcast_fusion.1 = f32[16384,256]{0,1:T(8,128)} fusion(bf16[2048,256]{1,0:T(8,128)(2,1)} %bitcast.24, bf16[16384,2048]{1,0:T(8,128)(2,1)} %bitcast.11), kind=kOutput, calls=%fused_computation.1 | convolution fusion | flops 17179869184 | bytes 84934656 | tf_op jit(solution)/shard_map/dot_general | solution.py:16
  89.0 17.4 %copy.15 = f32[16384,256]{1,0:T(8,128)} copy(f32[16384,256]{0,1:T(8,128)} %convolution_bitcast_fusion.1) | data formatting | bytes 33554432 | tf_op jit(solution)/shard_map/reshape | solution.py:39
  106.4 0.0 reduce-scatter.3.cloned.1.call-update
  106.4 0.2 reduce-scatter.5.cloned.1.call-start
  106.7 0.0 all-gather.7.cloned.1.call-done
  106.7 37.2 %convolution_bitcast_fusion = f32[16384,256]{0,1:T(8,128)} fusion(bf16[2048,256]{1,0:T(8,128)(2,1)} %bitcast.23, bf16[16384,2048]{1,0:T(8,128)(2,1)} %bitcast.11), kind=kOutput, calls=%fused_computation | convolution fusion | flops 17179869184 | bytes 84934656 | tf_op jit(solution)/shard_map/dot_general | solution.py:16
  143.9 17.5 %copy.16 = f32[16384,256]{1,0:T(8,128)} copy(f32[16384,256]{0,1:T(8,128)} %convolution_bitcast_fusion) | data formatting | bytes 33554432 | tf_op jit(solution)/shard_map/reshape | solution.py:39
  161.4 0.0 reduce-scatter.5.cloned.1.call-update
  161.4 0.1 dynamic-slice_bitcast_fusion
  161.5 126.3 %reduce-scatter.3.cloned.1.call-done = f32[64,16,256]{2,1,0:T(8,128)} async-done(((f32[64,256,256]{2,1,0:T(8,128)}), f32[64,16,256]{2,1,0:T(8,128)}) %reduce-scatter.3.cloned.1.call-update) | async-done | bytes 1048592 | tf_op jit(solution)/shard_map/reduce_scatter | solution.py:38
  287.8 181.5 %reduce-scatter.5.cloned.1.call-done = f32[64,16,256]{2,1,0:T(8,128)} async-done(((f32[64,256,256]{2,1,0:T(8,128)}), f32[64,16,256]{2,1,0:T(8,128)}) %reduce-scatter.5.cloned.1.call-update) | async-done | bytes 1048592 | tf_op jit(solution)/shard_map/reduce_scatter | solution.py:38
  469.3 1.8 fusion
  471.2 3.2 copy.14
Async XLA Ops:
  6.5 49.9 %all-gather.5.cloned.1.call-start = ((), (), s32[]{:S(2)}) async-start(), calls=%async_computation.4 | async-start | bytes 1572864 | tf_op jit(solution)/shard_map/all_gather | solution.py:35
  10.8 95.9 %all-gather.7.cloned.1.call-start = ((), (), s32[]{:S(2)}) async-start(), calls=%async_computation.5 | async-start | bytes 1572864 | tf_op jit(solution)/shard_map/all_gather | solution.py:35
  11.6 276.3 %reduce-scatter.3.cloned.1.call-start = ((), (), s32[]{:S(2)}) async-start(), calls=%async_computation.2 | async-start | bytes 17825792 | tf_op jit(solution)/shard_map/reduce_scatter | solution.py:38
  106.4 362.9 %reduce-scatter.5.cloned.1.call-start = ((), (), s32[]{:S(2)}) async-start(), calls=%async_computation.3 | async-start | bytes 17825792 | tf_op jit(solution)/shard_map/reduce_scatter | solution.py:38
Sparse Core Ops, SparseCore 0:
  10.9 23.9 all-gather.4
  36.5 21.2 all-gather.6
  106.6 181.2 reduce-scatter.2
  291.8 177.5 reduce-scatter.4
where the time goes:
time: 482 us; the launch traced here: 481 us
  waiting for transfers between devices  309 us (64%)
  local copies, waits for them, and re-layouts  84.3 us (17%)
  matrix products  69.7 us (14%)
  between operations  13.2 us (3%)
  other arithmetic  4.88 us (1%)
    reduce_scatter x2, waiting for transfers between devices, per_device(): lax.psum_scatter(partial_value.reshape(local_rows, width, width), 'row',...  308 us
    dot_general x2, matrix products, panel_product(): return jnp.dot(left, right, preferred_element_type=jnp.float32)  69.7 us
    unnamed x1, local copies, waits for them, and re-layouts  44.9 us
    reshape x2, local copies, waits for them, and re-layouts, per_device(): partial_value.reshape(local_rows, width, width)  35 us
  transfers between devices with their start and end apart: 4, of which 2 were waited for; matrix products, arithmetic and copies ran while one was open for 31% of the time, Pallas kernels for 0%

commit v1 on v0

--- a/solution.py
+++ b/solution.py
@@ -1,7 +1,16 @@
+import functools
+
 import jax
 import jax.numpy as jnp
 from jax import lax
+from jax.experimental import pallas as pl
+from jax.experimental.pallas import tpu as pltpu
 from jax.sharding import PartitionSpec as P
+
+MESH_IDS = pl.DeviceIdType.MESH
+STEP = 4
+RING = 8
+TOP = 32766.0
 
 
 def membership(ancestors, valid_flags, block_slot):
@@ -16,7 +25,7 @@
     return jnp.dot(left, right, preferred_element_type=jnp.float32)
 
 
-def per_device(inverse_tiles, factor_panels, ancestors, valid_flags, block_slot):
+def plain_device(inverse_tiles, factor_panels, ancestors, valid_flags, block_slot):
     local_rows = inverse_tiles.shape[0]
     width = inverse_tiles.shape[1]
     local_cols = inverse_tiles.shape[2]
@@ -44,9 +53,361 @@
     return jnp.where(rowmask, -stacked, jnp.zeros((), jnp.float32))
 
 
+def fused_kernel(
+    dims, order_ref, slot_ref, rowm_ref, colm_ref, panel_ref, left_ref, out_ref,
+    left_buf, left_sem, left_mat, right_mat, other_panel, part,
+    send_a, recv_a, sscale_a, rscale_a, keep_b, send_b, recv_b, sscale_b, rscale_b,
+    keep_c, send_c, recv_c, sscale_c, rscale_c, result,
+    panel_sems, a_ss, a_rs, as_ss, as_rs, b_ss, b_rs, bs_ss, bs_rs, c_ss, c_rs, cs_ss, cs_rs,
+):
+    n_outer, width, n_cols, panels, local_rows, cap, ring = dims
+    pairs = local_rows * panels
+    tiles = STEP // panels
+    lag = (pairs - cap) // STEP
+    steps = cap // STEP
+    m_steps = pairs // STEP
+    chunk = width // (4 * n_outer)
+    half = width // 2
+    quarter = width // 4
+    load_rows = tiles * width * n_cols
+
+    row = lax.axis_index("row")
+    col = lax.axis_index("col")
+    core = row % 2
+    mid = (row // 2) % 2
+    outer = row // 4
+    sibling = (row + 1 - 2 * core, col)
+    across = (row + 2 - 4 * mid, col)
+    others = [(((outer + d) % n_outer) * 4 + mid * 2 + core, col) for d in range(1, n_outer)]
+    twin = (row, 1 - col)
+
+    barrier = pltpu.get_barrier_semaphore()
+    for device in [sibling, across, twin] + others:
+        pl.semaphore_signal(barrier, inc=1, device_id=device, device_id_type=MESH_IDS)
+
+    def load(m):
+        return pltpu.make_async_copy(
+            left_ref.at[pl.ds(pl.multiple_of(m * load_rows, load_rows), load_rows)],
+            left_buf.at[m % 3], left_sem.at[m % 3],
+        )
+
+    load(0).start()
+    load(1).start()
+    pl.semaphore_wait(barrier, 2 + n_outer)
+
+    def remote(src, dst, ss, rs, device):
+        return pltpu.make_async_remote_copy(
+            src_ref=src, dst_ref=dst, send_sem=ss, recv_sem=rs, device_id=device, device_id_type=MESH_IDS
+        )
+
+    panel_copy = remote(panel_ref, other_panel, panel_sems.at[0], panel_sems.at[1], twin)
+    panel_copy.start()
+
+    deep = width // 2
+
+    def place(source, which_col):
+        for b in range(n_cols):
+            for s in range(panels):
+                block = source[s, b]
+                block = jnp.where(colm_ref[s * n_cols + b] > 0, block.astype(jnp.float32), 0.0)
+                start = pl.multiple_of(b * width + which_col * deep, deep)
+                right_mat[pl.ds(start, deep), pl.ds(s * width, width)] = block.astype(jnp.bfloat16)
+
+    place(panel_ref, col)
+    panel_copy.wait()
+    place(other_panel, 1 - col)
+
+    def copy_a(t):
+        return [
+            remote(send_a.at[t % 2], recv_a.at[t % RING], a_ss.at[t % 2], a_rs.at[t % RING], sibling),
+            remote(sscale_a.at[t % 2], rscale_a.at[t % RING], as_ss.at[t % 2], as_rs.at[t % RING], sibling),
+        ]
+
+    def copy_b(t):
+        return [
+            remote(send_b.at[t % 2], recv_b.at[t % RING], b_ss.at[t % 2], b_rs.at[t % RING], across),
+            remote(sscale_b.at[t % 2], rscale_b.at[t % RING], bs_ss.at[t % 2], bs_rs.at[t % RING], across),
+        ]
+
+    def copy_c(t, d):
+        return [
+            remote(send_c.at[t % 2, d], recv_c.at[t % RING, d], c_ss.at[d, t % 2], c_rs.at[d, t % RING], others[d]),
+            remote(sscale_c.at[t % 2], rscale_c.at[t % RING, d], cs_ss.at[d, t % 2], cs_rs.at[d, t % RING], others[d]),
+        ]
+
+    def multiply(m):
+        @pl.when(m + 2 < m_steps)
+        def _():
+            load(m + 2).start()
+
+        load(m).wait()
+        for g in range(tiles):
+            rows = width * n_cols
+            band = 32
+            for q in range(width // band):
+                piece = left_buf[m % 3, pl.ds(g * rows + q * band * n_cols, band * n_cols), :]
+                piece = piece.astype(jnp.float32).reshape(band, n_cols, width)
+                piece = jnp.swapaxes(piece, 0, 1).astype(jnp.bfloat16)
+                for b in range(n_cols):
+                    left_mat[
+                        pl.ds(g * width + q * band, band), pl.ds(b * width, width)
+                    ] = piece[b]
+        got = jnp.dot(left_mat[...], right_mat[...], preferred_element_type=jnp.float32)
+        base = (m * STEP) % ring
+        for g in range(tiles):
+            for s in range(panels):
+                for o in range(n_outer):
+                    for y in range(2):
+                        for c in range(2):
+                            r0 = g * width + ((o * 2 + y) * 2 + c) * chunk
+                            part[base + g * panels + s, c, y, pl.ds(o * chunk, chunk), :] = got[
+                                r0:r0 + chunk, s * width:(s + 1) * width
+                            ]
+
+    def stage_a(t):
+        @pl.when(t >= 2)
+        def _():
+            for c in copy_a(t):
+                c.wait_send()
+
+        top = jnp.zeros((1, width), jnp.float32)
+        for k in range(STEP):
+            at = order_ref[t * STEP + k]
+            for y in range(2):
+                value = part[at, 1 - core, y]
+                top = jnp.maximum(top, jnp.max(jnp.abs(value), axis=0, keepdims=True))
+        top = jnp.maximum(top, 1e-30)
+        scale = TOP / top
+        for k in range(STEP):
+            at = order_ref[t * STEP + k]
+            for y in range(2):
+                value = part[at, 1 - core, y]
+                send_a[t % 2, k, y] = jnp.round(value * scale).astype(jnp.int32).astype(jnp.int16)
+        sscale_a[t % 2] = jnp.broadcast_to(top * (1.0 / TOP), (8, width))
+        for c in copy_a(t):
+            c.start()
+
+    def stage_b(t):
+        @pl.when(t >= 2)
+        def _():
+            for c in copy_b(t):
+                c.wait_send()
+
+        for c in copy_a(t):
+            c.wait_recv()
+        unit = rscale_a[t % RING, pl.ds(0, 1), :]
+
+        def arrived(k, y):
+            return unit * recv_a[t % RING, k, y].astype(jnp.int32).astype(jnp.float32)
+
+        top = jnp.zeros((1, width), jnp.float32)
+        away = []
+        for k in range(STEP):
+            at = order_ref[t * STEP + k]
+            keep_b[t % 4, k] = part[at, core, mid] + arrived(k, mid)
+            value = part[at, core, 1 - mid] + arrived(k, 1 - mid)
+            away.append(value)
+            top = jnp.maximum(top, jnp.max(jnp.abs(value), axis=0, keepdims=True))
+        top = jnp.maximum(top, 1e-30)
+        scale = TOP / top
+        for k in range(STEP):
+            send_b[t % 2, pl.ds(k * quarter, quarter), :] = (
+                jnp.round(away[k] * scale).astype(jnp.int32).astype(jnp.int16)
+            )
+        sscale_b[t % 2] = jnp.broadcast_to(top * (1.0 / TOP), (8, width))
+        for c in copy_b(t):
+            c.start()
+
+    def stage_c(t):
+        @pl.when(t >= 2)
+        def _():
+            for d in range(n_outer - 1):
+                for c in copy_c(t, d):
+                    c.wait_send()
+
+        for c in copy_b(t):
+            c.wait_recv()
+        unit = rscale_b[t % RING, pl.ds(0, 1), :]
+        top = jnp.zeros((1, width), jnp.float32)
+        for k in range(STEP):
+            value = keep_b[t % 4, k] + unit * recv_b[
+                t % RING, pl.ds(k * quarter, quarter), :
+            ].astype(jnp.int32).astype(jnp.float32)
+            keep_c[t % 4, k] = value
+            top = jnp.maximum(top, jnp.max(jnp.abs(value), axis=0, keepdims=True))
+        top = jnp.maximum(top, 1e-30)
+        scale = TOP / top
+        for d in range(n_outer - 1):
+            goal = (outer + d + 1) % n_outer
+            for k in range(STEP):
+                value = keep_c[t % 4, k, pl.ds(pl.multiple_of(goal * chunk, chunk), chunk), :]
+                send_c[t % 2, d, pl.ds(k * chunk, chunk), :] = (
+                    jnp.round(value * scale).astype(jnp.int32).astype(jnp.int16)
+                )
+        sscale_c[t % 2] = jnp.broadcast_to(top * (1.0 / TOP), (8, width))
+        for d in range(n_outer - 1):
+            for c in copy_c(t, d):
+                c.start()
+
+    def stage_d(t):
+        for d in range(n_outer - 1):
+            for c in copy_c(t, d):
+                c.wait_recv()
+        for k in range(STEP):
+            value = keep_c[t % 4, k, pl.ds(pl.multiple_of(outer * chunk, chunk), chunk), :]
+            for d in range(n_outer - 1):
+                unit = rscale_c[t % RING, d, pl.ds(0, 1), :]
+                value = value + unit * recv_c[
+                    t % RING, d, pl.ds(k * chunk, chunk), :
+                ].astype(jnp.int32).astype(jnp.float32)
+            result[t * STEP + k] = -value
+
+    def body(it, carry):
+        t = it - lag
+
+        @pl.when(it < m_steps)
+        def _():
+            multiply(it)
+
+        @pl.when((t - 2 >= 0) & (t - 2 < steps))
+        def _():
+            stage_b(t - 2)
+
+        @pl.when((t - 4 >= 0) & (t - 4 < steps))
+        def _():
+            stage_c(t - 4)
+
+        @pl.when((t - 6 >= 0) & (t - 6 < steps))
+        def _():
+            stage_d(t - 6)
+
+        @pl.when((t >= 0) & (t < steps))
+        def _():
+            stage_a(t)
+
+        return carry
+
+    lax.fori_loop(0, m_steps + 6, body, 0)
+    for last in (steps - 2, steps - 1):
+        for c in copy_a(last):
+            c.wait_send()
+        for c in copy_b(last):
+            c.wait_send()
+        for d in range(n_outer - 1):
+            for c in copy_c(last, d):
+                c.wait_send()
+
+    def write(i, carry):
+        for s in range(panels):
+            p = i * panels + s
+            value = result[slot_ref[p]]
+            out_ref[s, i] = jnp.where(rowm_ref[p] > 0, value, 0.0)
+        return carry
+
+    lax.fori_loop(0, local_rows, write, 0)
+
+
+def fused_call(cap, number, n_row, local_rows, width, n_cols, panels, row_flags, col_flags, left, factor_panels):
+    pairs = local_rows * panels
+    n_outer = n_row // 4
+    chunk = width // n_row
+    half, quarter = width // 2, width // 4
+    ring = pairs - cap + 4 * STEP
+    spot = jnp.arange(pairs, dtype=jnp.int32)
+    before = (spot[None, :] < spot[:, None]) & (row_flags[None, :] > 0)
+    rank = jnp.sum(before.astype(jnp.int32), axis=1)
+    slot = jnp.maximum(rank, spot - (pairs - cap))
+    slot_used = jnp.where(row_flags > 0, slot, 0)
+    places = jnp.arange(cap, dtype=jnp.int32)
+    hit = (slot[None, :] == places[:, None]) & (row_flags[None, :] > 0)
+    order = places + jnp.sum(jnp.where(hit, spot[None, :] - places[:, None], 0), axis=1)
+    order = order % ring
+    load_rows = (STEP // panels) * width * n_cols
+    f32, bf16, i16 = jnp.float32, jnp.bfloat16, jnp.int16
+    dma = pltpu.SemaphoreType.DMA
+    smem = pl.BlockSpec(memory_space=pltpu.SMEM)
+    vmem = pl.BlockSpec(memory_space=pltpu.VMEM)
+    out = pl.pallas_call(
+        functools.partial(fused_kernel, (n_outer, width, n_cols, panels, local_rows, cap, ring)),
+        out_shape=jax.ShapeDtypeStruct((panels, local_rows, chunk, width), f32),
+        in_specs=[smem, smem, smem, smem, vmem, pl.BlockSpec(memory_space=pl.ANY)],
+        out_specs=vmem,
+        scratch_shapes=[
+            pltpu.VMEM((3, load_rows, width), bf16),
+            dma((3,)),
+            pltpu.VMEM(((STEP // panels) * width, n_cols * width), bf16),
+            pltpu.VMEM((n_cols * width, panels * width), bf16),
+            pltpu.VMEM(factor_panels.shape, bf16),
+            pltpu.VMEM((ring, 2, 2, quarter, width), f32),
+            pltpu.VMEM((2, STEP, 2, quarter, width), i16),
+            pltpu.VMEM((RING, STEP, 2, quarter, width), i16),
+            pltpu.VMEM((2, 8, width), f32),
+            pltpu.VMEM((RING, 8, width), f32),
+            pltpu.VMEM((4, STEP, quarter, width), f32),
+            pltpu.VMEM((2, STEP * quarter, width), i16),
+            pltpu.VMEM((RING, STEP * quarter, width), i16),
+            pltpu.VMEM((2, 8, width), f32),
+            pltpu.VMEM((RING, 8, width), f32),
+            pltpu.VMEM((4, STEP, quarter, width), f32),
+            pltpu.VMEM((2, n_outer - 1, STEP * chunk, width), i16),
+            pltpu.VMEM((RING, n_outer - 1, STEP * chunk, width), i16),
+            pltpu.VMEM((2, 8, width), f32),
+            pltpu.VMEM((RING, n_outer - 1, 8, width), f32),
+            pltpu.VMEM((cap, chunk, width), f32),
+            dma((2,)),
+            dma((2,)), dma((RING,)), dma((2,)), dma((RING,)),
+            dma((2,)), dma((RING,)), dma((2,)), dma((RING,)),
+            dma((n_outer - 1, 2)), dma((n_outer - 1, RING)),
+            dma((n_outer - 1, 2)), dma((n_outer - 1, RING)),
+        ],
+        compiler_params=pltpu.CompilerParams(
+            collective_id=number, has_side_effects=True, vmem_limit_bytes=56 * 1024 * 1024
+        ),
+    )(order, slot_used, row_flags, col_flags, factor_panels, left)
+    return out
+
+
+def per_device(n_row, inverse_tiles, factor_panels, ancestors, valid_flags, block_slot):
+    local_rows, width, n_cols, _ = inverse_tiles.shape
+    panels = factor_panels.shape[0]
+    pairs = local_rows * panels
+    member = membership(ancestors, valid_flags, block_slot)
+    halves = member.reshape(panels, -1, local_rows)
+    count = jnp.max(jnp.sum(halves.astype(jnp.int32), axis=(0, 2)))
+    col_start = lax.axis_index("row") * n_cols
+    row_start = lax.axis_index("col") * local_rows
+    col_flags = lax.dynamic_slice_in_dim(member, col_start, n_cols, 1).astype(jnp.int32).reshape(-1)
+    row_flags = jnp.transpose(
+        lax.dynamic_slice_in_dim(member, row_start, local_rows, 1)
+    ).astype(jnp.int32).reshape(-1)
+    left = inverse_tiles.reshape(local_rows * width * n_cols, width)
+    caps = CAPS(pairs)
+    calls = [
+        functools.partial(fused_call, cap, k, n_row, local_rows, width, n_cols, panels)
+        for k, cap in enumerate(caps)
+    ]
+    args = (row_flags, col_flags, left, factor_panels)
+    if len(calls) == 1:
+        out = calls[0](*args)
+    else:
+        which = sum((count > cap).astype(jnp.int32) for cap in caps[:-1])
+        out = lax.switch(which, calls, *args)
+    return jnp.transpose(out, (1, 2, 0, 3))
+
+
+def CAPS(pairs):
+    return [pairs]
+
+
+def fits(mesh):
+    n_row, n_col = mesh.shape["row"], mesh.shape["col"]
+    return n_col == 2 and n_row % 4 == 0 and n_row <= 16
+
+
 def solution(mesh):
+    body = functools.partial(per_device, mesh.shape["row"]) if fits(mesh) else plain_device
     return jax.shard_map(
-        per_device,
+        body,
         mesh=mesh,
         in_specs=(P("col", None, "row", None), P(None, "row", "col", None), P(), P(), P()),
         out_specs=P("col", "row", None, None),

time: 482 us -> 167 us (0.35)
  waiting for transfers between devices: 309 us -> 0 us
  Pallas kernels: 0 us -> 158 us
  local copies, waits for them, and re-layouts: 84.3 us -> 5.67 us
  matrix products: 69.7 us -> 0 us
  between operations: 13.2 us -> 0.04 us
    reduce_scatter x2 -> x0, waiting for transfers between devices: 308 us -> none  [per_device(): lax.psum_scatter(partial_value.reshape(local_rows, width, width), 'row',...]
    pallas_call x0 -> x1, Pallas kernels: none -> 158 us  [fused_call(): pl.pallas_call(functools.partial(fused_kernel, (n_outer, width, n_cols, p...]
    dot_general x2 -> x0, matrix products: 69.7 us -> none  [panel_product(): return jnp.dot(left, right, preferred_element_type=jnp.float32)]
    unnamed x1 -> x2, local copies, waits for them, and re-layouts: 44.9 us -> 0.01 us
    reshape x2 -> x1, local copies, waits for them, and re-layouts: 35 us -> 0.61 us  [per_device(): lax.dynamic_slice_in_dim(member, col_start, n_cols, 1).astype(jnp.int32)]
  transfers between devices with their start and end apart: 4 -> 0, of which waited for: 2 -> 0; matrix products, arithmetic and copies ran while one was open for 31% -> 0% of each run, Pallas kernels for 0% -> 0%
where the time goes in v1:
time: 167 us
  Pallas kernels  158 us (95%)
  local copies, waits for them, and re-layouts  5.67 us (3%)
  other arithmetic  3.12 us (2%)
    pallas_call x1, Pallas kernels, fused_call(): pl.pallas_call(functools.partial(fused_kernel, (n_outer, width, n_cols, p...  158 us
    transpose x1, local copies, waits for them, and re-layouts, per_device(): return jnp.transpose(out, (1, 2, 0, 3))  4.82 us

profile of v1, /device:TPU:0, one launch (start us, length us, event | category | flops | bytes accessed | tf_op | source)
XLA Modules:
  0.0 166.9 jit_solution(3094503531262354811)
XLA Ops:
  0.0 0.7 broadcast_compare_fusion
  0.7 0.9 select_reduce_fusion
  1.6 0.1 fusion.1
  1.7 0.1 dynamic-slice_convert_fusion
  1.8 0.6 reshape.33.colm_ref
  2.4 0.1 fusion.4
  2.5 0.1 copy.10
  2.6 0.1 reshape.31.rowm_ref
  2.7 0.0 copy-start
  2.7 0.1 convert_reduce_fusion
  2.8 0.5 broadcast_select_fusion
  3.3 0.1 select_reduce_fusion.1
  3.5 0.5 and_select_fusion.order_ref
  4.0 0.0 copy-done
  4.0 158.0 %shard_map.55 = f32[2,64,16,256]{3,2,1,0:T(8,128)} custom-call(s32[128]{0:T(128)} %and_select_fusion.order_ref, s32[128]{0:T(128)} %get-tuple-element.5.slot_ref, s32[128]{0:T(128)} %copy-done, s32[16]{0:T(128)} %reshape.33.colm_ref, bf16[2,8,128,256]{3,2,1,0:T(8,128)(2,1)} %panel_ref.1, bf16[131072,256]{1,0:T(8,128)(2,1)} %bitcast.1.left_ref), custom_call_target="tpu_custom_call" | custom-call | tf_op jit(solution)/shard_map/pallas_call | solution.py:330
  162.0 4.8 %copy.11 = f32[64,16,2,256]{3,2,1,0:T(2,128)} copy(f32[64,16,2,256]{3,1,0,2:T(8,128)} %bitcast.4) | data formatting | bytes 4194304 | tf_op jit(solution)/shard_map/transpose | solution.py:395
  (1 shorter events, 0.0 us)
Async XLA Ops:
  2.7 1.3 copy-start
